TPU v7x, 32 devices: a whole 2x2x4 slice. The times are simulated.
32 devices in a mesh: groups: 2 (over y), dp: 4 (over z), mp: 4 (over x, core).
Axes of the slice: x: 2, y: 2, z: 4, core: 2. Of those that a mesh axis runs over, the one named last changes fastest.
Arguments:
- replay_obs: bfloat16 [256, 16, 2048], P(('groups', 'dp'), None, 'mp'), parts along dimension 0, may hold values from -6 to 6
- priorities: int32 [256], P(('groups', 'dp')), parts along dimension 0, may hold values from 16 to 191, as said below
- sample_owner: int32 [256, 1], P(('groups', 'dp')), parts along dimension 0, may hold values from 0 to 3; in each aligned block of 32 rows (0 to 31, 32 to 63, ...) at most 16 rows name the same one
- sample_slot: int32 [256], P(('groups', 'dp')), parts along dimension 0, may hold values from 0 to 31
- cotangent: bfloat16 [4096, 2048], P(('groups', 'dp'), 'mp'), parts along dimension 0, may hold values from -0.39648438 to 0.39648438
- norm_gain: float32 [2048], replicated, may hold values from 0.5 to 1.5
- w_in: bfloat16 [2048, 4096], P(None, 'mp'), may hold values from -0.125 to 0.125
- w_out: bfloat16 [2048, 4096], P(None, 'mp'), may hold values from -0.09375 to 0.09375
Outputs:
- grad_in: bfloat16 [4096, 4096], P(('groups', 'dp'), 'mp'), parts along dimension 0
- grad_out: bfloat16 [4096, 4096], P(('groups', 'dp'), 'mp'), parts along dimension 0
There are 2 independent parts, one for each index of `groups`. A program takes and returns all parts, laid end to end along the dimension named above; an argument that names none is the same for every part. Nothing has to cross between parts.
Inputs may be any that keep to these rules, and one draw needn't show every extreme that they name: `sample_owner`: within the 32 samples of one learner no replay shard is named more than 16 times; in every draw some learner names one shard exactly 16 times. `priorities`: priorities are whole numbers; the smallest and the largest stated are reached in every draw.
All inputs are finite; a program needn't handle non-finite values.
Results may differ from a plain program's by a relative error of at most 0.012.
Values may be sent and summed in bfloat16 or wider, within the bound.
A program may use at most 128 MiB of HBM per device.

v0:
```python
import functools

import jax
import jax.numpy as jnp
from jax import lax
from jax.experimental import pallas as pl
from jax.experimental.pallas import tpu as pltpu
from jax.sharding import PartitionSpec as P

MESH = pl.DeviceIdType.MESH

priority_exponent = 0.6
norm_epsilon = 1e-05
root_two_over_pi = 0.7978845608028654


def gelu_tanh(inputs):
    inner = root_two_over_pi * (inputs + 0.044715 * inputs * inputs * inputs)
    return 0.5 * inputs * (1.0 + jnp.tanh(inner))


def gelu_slope(inputs):
    inner = root_two_over_pi * (inputs + 0.044715 * inputs * inputs * inputs)
    tangent = jnp.tanh(inner)
    return 0.5 * (1.0 + tangent) + 0.5 * inputs * (1.0 - tangent * tangent) * root_two_over_pi * (
        1.0 + 3.0 * 0.044715 * inputs * inputs
    )


def contract_rows(left, right):
    return lax.dot_general(
        left, right, (((0,), (0,)), ((), ())), preferred_element_type=jnp.float32
    )


def backward_hidden(upstream, w_out, pre_act):
    d_hidden = jnp.dot(upstream, w_out, preferred_element_type=jnp.float32)
    return (d_hidden * gelu_slope(pre_act)).astype(jnp.bfloat16)


def body(replay_obs, priorities, sample_owner, sample_slot, cotangent, norm_gain, w_in, w_out):
    shards = lax.axis_size("dp")
    owners = sample_owner[:, 0]
    samples = owners.shape[0]
    capacity = max(2, 2 * samples // shards)
    seg_len = replay_obs.shape[1]
    feature_cols = replay_obs.shape[2]
    order = jnp.arange(samples, dtype=jnp.int32)
    earlier = (owners[:, None] == owners[None, :]) & (order[None, :] < order[:, None])
    rank_in = jnp.sum(earlier.astype(jnp.int32), axis=1)
    position = owners * capacity + rank_in
    table = jnp.arange(shards * capacity, dtype=jnp.int32)
    hits = position[:, None] == table[None, :]
    requests = jnp.sum(jnp.where(hits, sample_slot[:, None], 0), axis=0).reshape(shards, capacity)
    asked = lax.all_to_all(requests, "dp", split_axis=0, concat_axis=0, tiled=True)
    flat = asked.reshape(-1)
    rows_out = jnp.take(replay_obs, flat, axis=0).reshape(asked.shape + (seg_len, feature_cols))
    level_out = (
        jnp.take(priorities, flat).astype(jnp.float32).astype(jnp.bfloat16).reshape(asked.shape)
    )
    arrived = lax.all_to_all(rows_out, "dp", split_axis=0, concat_axis=0, tiled=True)
    arrived_levels = lax.all_to_all(level_out, "dp", split_axis=0, concat_axis=0, tiled=True)
    observed = jnp.take(arrived.reshape(shards * capacity, seg_len, feature_cols), position, axis=0)
    observed = observed.reshape(samples * seg_len, feature_cols)
    levels = jnp.take(arrived_levels.reshape(-1), position).astype(jnp.float32)
    raw_weight = jnp.power(levels, -priority_exponent)
    largest = lax.pmax(jnp.max(raw_weight), "dp")
    whole_obs, whole_cot = (
        lax.all_gather(observed, "mp", axis=1, tiled=True),
        lax.all_gather(cotangent, "mp", axis=1, tiled=True),
    )
    inputs32 = whole_obs.astype(jnp.float32)
    mean_square = jnp.mean(inputs32 * inputs32, axis=1, keepdims=True)
    normed = (inputs32 * lax.rsqrt(mean_square + norm_epsilon) * norm_gain).astype(jnp.bfloat16)
    pre_act = jnp.dot(normed, w_in, preferred_element_type=jnp.float32)
    hidden = gelu_tanh(pre_act).astype(jnp.bfloat16)
    token_weight = jnp.repeat(raw_weight, seg_len)
    upstream = (whole_cot.astype(jnp.float32) * token_weight[:, None]).astype(jnp.bfloat16)
    hidden_cols = w_in.shape[1]
    d_pre = backward_hidden(upstream, w_out, pre_act)
    term_in = contract_rows(normed, d_pre)
    summed = lax.psum_scatter(
        jnp.concatenate([term_in, contract_rows(upstream, hidden)], axis=1).astype(jnp.bfloat16),
        "dp",
        scatter_dimension=0,
        tiled=True,
    ).astype(jnp.float32)
    grad_in_sum = summed[:, :hidden_cols]
    grad_out_sum = summed[:, hidden_cols:]
    return (
        (grad_in_sum / largest).astype(jnp.bfloat16),
        (grad_out_sum / largest).astype(jnp.bfloat16),
    )


SHARDS = 4
PARTS = 4
LEAD = 2
OWNER_AT, SLOT_AT, LEVEL_AT = 0, 32, 64


def gather_kernel(
    chunk, seg_len, meta_ref, gain_ref, obs_ref, cot_ref, win_ref, wout_ref, gin_ref, gout_ref,
    buf, win, wout, hidden_r, slope_r, normed_r, hidden_g, slope_g, normed_g, normed_t, wt,
    acc_in, acc_out, meta_all, weight_v, meta_s, weight_s,
    local_sem, meta_send, meta_recv, zr_send, zl_send, z_recv, x_send, x_recv, c1_send, c1_recv,
    c2_send, c2_recv,
):
    rows, cols = obs_ref.shape
    pieces = rows // chunk
    segs = rows // seg_len
    chunk_segs = chunk // seg_len
    events = 2 * SHARDS * pieces
    half = events // 2
    width = win.shape[1]
    g, z, m = lax.axis_index("groups"), lax.axis_index("dp"), lax.axis_index("mp")
    core, across = m % 2, m // 2
    mate = 2 * across + (1 - core)
    far = 2 * (1 - across) + core
    mate_far = 2 * (1 - across) + (1 - core)
    toward = 1 - 2 * (z // 2)
    inner = ((z + 1) // 2) % 2

    def split(e):
        return e // half, (e // pieces) % SHARDS, e % pieces

    def shard_at(k):
        return z + toward * (k - inner * (k // 2) * (3 - 2 * (k % 2)))

    def block(a, s, c, column):
        return buf.at[
            a,
            pl.ds(pl.multiple_of(s * rows + c * chunk, chunk), chunk),
            pl.ds(pl.multiple_of(column * cols, cols), cols),
        ]

    def move(a, s, c, column, send, recv, target):
        at = (a * SHARDS + s) * pieces + c
        part = block(a, s, c, column)
        return pltpu.make_async_remote_copy(
            src_ref=part, dst_ref=part, send_sem=send.at[at], recv_sem=recv.at[at],
            device_id=target, device_id_type=MESH,
        )

    def along(a, s, c, step):
        return move(a, s, c, m, zr_send if step > 0 else zl_send, z_recv, (g, z + step, m))

    def over_x(a, s, c, column):
        return move(a, s, c, column, x_send, x_recv, (g, z, far))

    def to_mate(a, s, c, column):
        return move(a, s, c, column, c1_send, c1_recv, (g, z, mate))

    def pass_on(a, s, c, column):
        return move(a, s, c, column, c2_send, c2_recv, (g, z, mate))

    def inside(s):
        return jnp.logical_and(s >= 0, s < SHARDS)

    def launch(e):
        a, k, c = split(e)
        for step in (1, -1):
            s = z - step * k

            @pl.when(jnp.logical_and(inside(s), k > 0))
            def _():
                along(a, s, c, step).wait_recv()

            @pl.when(jnp.logical_and(inside(s), inside(z + step)))
            def _():
                along(a, s, c, step).start()

        s = shard_at(k)
        over_x(a, s, c, m).start()
        to_mate(a, s, c, m).start()

    def finish(e):
        a, k, c = split(e)
        for step in (1, -1):
            s = z - step * k

            @pl.when(jnp.logical_and(inside(s), inside(z + step)))
            def _():
                along(a, s, c, step).wait_send()

        s = shard_at(k)
        over_x(a, s, c, m).wait_send()
        to_mate(a, s, c, m).wait_send()
        pass_on(a, s, c, far).wait_send()

    def arrive(e):
        a, k, c = split(e)
        s = shard_at(k)
        over_x(a, s, c, far).wait_recv()
        pass_on(a, s, c, far).start()
        to_mate(a, s, c, mate).wait_recv()
        pass_on(a, s, c, mate_far).wait_recv()
        return s, c

    own_rows = pl.ds(pl.multiple_of(z * rows, rows), rows)
    own_cols = pl.ds(pl.multiple_of(m * cols, cols), cols)
    out_cols = pl.ds(pl.multiple_of(z * cols, cols), cols)
    local = [
        pltpu.make_async_copy(obs_ref, buf.at[0, own_rows, own_cols], local_sem.at[0]),
        pltpu.make_async_copy(cot_ref, buf.at[1, own_rows, own_cols], local_sem.at[1]),
        pltpu.make_async_copy(win_ref, win, local_sem.at[2]),
        pltpu.make_async_copy(wout_ref, wout, local_sem.at[3]),
    ]
    for copy in local:
        copy.start()

    barrier = pltpu.get_barrier_semaphore()
    for target in [(g, (z + d) % SHARDS, m) for d in range(1, SHARDS)] + [(g, z, mate), (g, z, far)]:
        pl.semaphore_signal(barrier, inc=1, device_id=target, device_id_type=MESH)
    pl.semaphore_wait(barrier, SHARDS + 1)

    def tell(d, source):
        return pltpu.make_async_remote_copy(
            src_ref=meta_ref, dst_ref=meta_all.at[source], send_sem=meta_send.at[d - 1],
            recv_sem=meta_recv.at[source], device_id=(g, (z + d) % SHARDS, m), device_id_type=MESH,
        )

    for d in range(1, SHARDS):
        tell(d, z).start()
    local[0].wait()
    local[1].wait()
    for e in range(LEAD):
        launch(jnp.int32(e))
    meta_all[z] = meta_ref[...]
    acc_in[...] = jnp.zeros_like(acc_in)
    acc_out[...] = jnp.zeros_like(acc_out)
    for d in range(1, SHARDS):
        tell(d, (z + SHARDS - d) % SHARDS).wait_recv()
    weight_v[...] = jnp.exp(-priority_exponent * jnp.log(meta_all[...].astype(jnp.float32)))
    for copy in (
        pltpu.make_async_copy(meta_all, meta_s, local_sem.at[4]),
        pltpu.make_async_copy(weight_v, weight_s, local_sem.at[5]),
    ):
        copy.start()
        copy.wait()
    local[2].wait()
    local[3].wait()

    def forward(e, carry):
        launch(e + LEAD)
        s, c = arrive(e)
        first = pl.multiple_of(s * rows + c * chunk, chunk)
        for j in range(chunk_segs):
            weight = weight_s[s, 0, LEVEL_AT + c * chunk_segs + j]
            wt[j * seg_len : (j + 1) * seg_len, :] = jnp.full((seg_len, 128), weight, jnp.float32)

        def norm(t, carry):
            at = pl.multiple_of(t * 64, 64)
            x = buf[0, pl.ds(first + at, 64), :].astype(jnp.float32)
            scale = lax.rsqrt(jnp.mean(x * x, axis=1, keepdims=True) + norm_epsilon)
            normed_t[pl.ds(at, 64), :] = (x * scale * gain_ref[...]).astype(jnp.bfloat16)
            return carry

        lax.fori_loop(0, chunk // 64, norm, 0)
        seg0 = s * segs + c * chunk_segs
        normed_r[pl.ds(seg0, chunk_segs)] = normed_t[:, out_cols].reshape(chunk_segs, seg_len, cols)

        def tile(n, carry):
            at = pl.ds(pl.multiple_of(n * 256, 256), 256)
            u = jnp.dot(normed_t[...], win[:, at], preferred_element_type=jnp.float32)
            weight = wt[:, :1]
            square = u * u
            tangent = jnp.tanh(root_two_over_pi * u * (1.0 + 0.044715 * square))
            upper = 0.5 * weight * (1.0 + tangent)
            slope = upper * (
                1.0 + u * (1.0 - tangent) * (root_two_over_pi * (1.0 + 3.0 * 0.044715 * square))
            )
            hidden = (upper * u).astype(jnp.bfloat16)
            hidden_r[pl.ds(seg0, chunk_segs), :, at] = hidden.reshape(chunk_segs, seg_len, 256)
            slope_r[pl.ds(seg0, chunk_segs), :, at] = slope.reshape(chunk_segs, seg_len, 256)
            return carry

        lax.fori_loop(0, width // 256, tile, 0)
        return carry

    lax.fori_loop(0, half, forward, 0)

    def widest(i, best):
        b, j = i // segs, i % segs
        return jnp.maximum(
            best, weight_s[meta_s[b, 0, OWNER_AT + j], 0, LEVEL_AT + meta_s[b, 0, SLOT_AT + j]]
        )

    largest = lax.fori_loop(0, SHARDS * segs, widest, jnp.float32(0.0))

    def backward(e, carry):
        @pl.when(e + LEAD < events)
        def _():
            launch(e + LEAD)

        _, k, c0 = split(e)
        s0 = shard_at(k)

        def pick(j, carry):
            at = c0 * chunk_segs + j
            r = meta_s[s0, 0, OWNER_AT + at] * segs + meta_s[s0, 0, SLOT_AT + at]
            hidden_g[j] = hidden_r[r]
            slope_g[j] = slope_r[r]
            normed_g[j] = normed_r[r]
            return carry

        lax.fori_loop(0, chunk_segs, pick, 0)
        s, c = arrive(e)
        first = pl.multiple_of(s * rows + c * chunk, chunk)
        here = pl.ds(first, chunk)
        turned = normed_g[...].reshape(chunk, cols).T
        cot_turned = buf[1, here, out_cols].T

        def tile(n, carry):
            at = pl.ds(pl.multiple_of(n * 256, 256), 256)
            d_hidden = jnp.dot(buf[1, here, :], wout[:, at], preferred_element_type=jnp.float32)
            d_pre = (d_hidden * slope_g[:, :, at].reshape(chunk, 256)).astype(jnp.bfloat16)
            acc_in[:, at] += jnp.dot(turned, d_pre, preferred_element_type=jnp.float32)
            acc_out[:, at] += jnp.dot(
                cot_turned, hidden_g[:, :, at].reshape(chunk, 256),
                preferred_element_type=jnp.float32,
            )
            return carry

        lax.fori_loop(0, width // 256, tile, 0)
        return carry

    lax.fori_loop(half, events, backward, 0)
    gin_ref[...] = (acc_in[...] / largest).astype(jnp.bfloat16)
    gout_ref[...] = (acc_out[...] / largest).astype(jnp.bfloat16)

    def settle(e, carry):
        finish(e)
        return carry

    lax.fori_loop(0, events, settle, 0)
    for d in range(1, SHARDS):
        tell(d, z).wait_send()


def gathered_body(
    replay_obs, priorities, sample_owner, sample_slot, cotangent, norm_gain, w_in, w_out
):
    segs, seg_len, cols = replay_obs.shape
    rows = segs * seg_len
    depth, width = w_in.shape
    chunk = 256
    count = 2 * SHARDS * (rows // chunk)
    chunk_segs = chunk // seg_len
    meta = jnp.concatenate(
        [sample_owner[:, 0], sample_slot, priorities, jnp.ones((32,), jnp.int32)]
    )
    meta = jnp.broadcast_to(meta[None, :], (8, 128))
    anywhere = pl.BlockSpec(memory_space=pl.ANY)
    vmem = pl.BlockSpec(memory_space=pltpu.VMEM)
    bf16, f32 = jnp.bfloat16, jnp.float32
    total = SHARDS * segs
    return pl.pallas_call(
        functools.partial(gather_kernel, chunk, seg_len),
        out_shape=[jax.ShapeDtypeStruct((cols, width), bf16)] * 2,
        in_specs=[vmem, vmem, anywhere, anywhere, anywhere, anywhere],
        out_specs=[vmem, vmem],
        scratch_shapes=[
            pltpu.VMEM((2, SHARDS * rows, depth), bf16),
            pltpu.VMEM((depth, width), bf16),
            pltpu.VMEM((depth, width), bf16),
            pltpu.VMEM((total, seg_len, width), bf16),
            pltpu.VMEM((total, seg_len, width), f32),
            pltpu.VMEM((total, seg_len, cols), bf16),
            pltpu.VMEM((chunk_segs, seg_len, width), bf16),
            pltpu.VMEM((chunk_segs, seg_len, width), f32),
            pltpu.VMEM((chunk_segs, seg_len, cols), bf16),
            pltpu.VMEM((chunk, depth), bf16),
            pltpu.VMEM((chunk, 128), f32),
            pltpu.VMEM((cols, width), f32),
            pltpu.VMEM((cols, width), f32),
            pltpu.VMEM((SHARDS, 8, 128), jnp.int32),
            pltpu.VMEM((SHARDS, 8, 128), f32),
            pltpu.SMEM((SHARDS, 8, 128), jnp.int32),
            pltpu.SMEM((SHARDS, 8, 128), f32),
            pltpu.SemaphoreType.DMA((6,)),
            pltpu.SemaphoreType.DMA((SHARDS - 1,)),
            pltpu.SemaphoreType.DMA((SHARDS,)),
        ]
        + [pltpu.SemaphoreType.DMA((count,))] * 9,
        compiler_params=pltpu.CompilerParams(
            collective_id=0, has_side_effects=True, vmem_limit_bytes=58 * 1024 * 1024
        ),
        name="gathered_step",
    )(meta, norm_gain[None, :], replay_obs.reshape(rows, cols), cotangent, w_in, w_out)


def solution(mesh):
    fits = mesh.shape["dp"] == SHARDS and mesh.shape["mp"] == PARTS
    return jax.shard_map(
        gathered_body if fits else body,
        mesh=mesh,
        in_specs=(
            P(("groups", "dp"), None, "mp"),
            P(("groups", "dp")),
            P(("groups", "dp"), None),
            P(("groups", "dp")),
            P(("groups", "dp"), "mp"),
            P(),
            P(None, "mp"),
            P(None, "mp"),
        ),
        out_specs=(P(("groups", "dp"), "mp"), P(("groups", "dp"), "mp")),
        check_vma=False,
    )
```

profile of v0, /device:TPU:1, one launch (start us, length us, event | category | flops | bytes accessed | tf_op | source)
XLA Modules:
  0.0 116.3 jit_solution(13538258242112914651)
XLA Ops:
  0.6 0.8 pad_add_fusion
  1.4 0.6 broadcast_in_dim.13.meta_ref
  2.0 109.7 %gathered_step.1 = (bf16[512,1024]{1,0:T(8,128)(2,1)}, bf16[512,1024]{1,0:T(8,128)(2,1)}) custom-call(s32[8,128]{1,0:T(8,128)} %broadcast_in_dim.13.meta_ref, f32[1,2048]{1,0:T(1,128)} %bitcast.4, bf16[512,512]{1,0:T(8,128)(2,1)} %bitcast.3, bf16[512,512]{1,0:T(8,128)(2,1)} %cot_ref.1, bf16[2048,1024]{1,0:T(8,128)(2,1)} %win_ref.1, bf16[2048,1024]{1,0:T(8,128)(2,1)} %wout_ref.1), custom_call_target="tpu_custom_call" | custom-call | tf_op jit(solution)/shard_map/gathered_step/pallas_call | solution.py:358
  111.8 2.3 %copy.12 = bf16[512,1024]{1,0:T(8,128)(2,1)} copy(bf16[512,1024]{1,0:T(8,128)(2,1)} %get-tuple-element.4) | data formatting | bytes 2097152
  114.0 2.3 %copy.13 = bf16[512,1024]{1,0:T(8,128)(2,1)} copy(bf16[512,1024]{1,0:T(8,128)(2,1)} %get-tuple-element.5) | data formatting | bytes 2097152
  (1 shorter events, 0.0 us)
where the time goes:
time: 117 us; the launch traced here: 116 us
  Pallas kernels  110 us (94%)
  local copies, waits for them, and re-layouts  5.12 us (4%)
    pallas_call x1, Pallas kernels, gathered_body(): pl.pallas_call(functools.partial(gather_kernel, chunk, seg_len), out_shap...  110 us
    unnamed x2, local copies, waits for them, and re-layouts  4.52 us

commit v1 on v0

--- a/solution.py
+++ b/solution.py
@@ -261,7 +261,7 @@
         normed_r[pl.ds(seg0, chunk_segs)] = normed_t[:, out_cols].reshape(chunk_segs, seg_len, cols)
 
         def tile(n, carry):
-            at = pl.ds(pl.multiple_of(n * 256, 256), 256)
+            at = pl.ds(pl.multiple_of(n * 512, 512), 512)
             u = jnp.dot(normed_t[...], win[:, at], preferred_element_type=jnp.float32)
             weight = wt[:, :1]
             square = u * u
@@ -271,11 +271,11 @@
                 1.0 + u * (1.0 - tangent) * (root_two_over_pi * (1.0 + 3.0 * 0.044715 * square))
             )
             hidden = (upper * u).astype(jnp.bfloat16)
-            hidden_r[pl.ds(seg0, chunk_segs), :, at] = hidden.reshape(chunk_segs, seg_len, 256)
-            slope_r[pl.ds(seg0, chunk_segs), :, at] = slope.reshape(chunk_segs, seg_len, 256)
+            hidden_r[pl.ds(seg0, chunk_segs), :, at] = hidden.reshape(chunk_segs, seg_len, 512)
+            slope_r[pl.ds(seg0, chunk_segs), :, at] = slope.reshape(chunk_segs, seg_len, 512)
             return carry
 
-        lax.fori_loop(0, width // 256, tile, 0)
+        lax.fori_loop(0, width // 512, tile, 0)
         return carry
 
     lax.fori_loop(0, half, forward, 0)
@@ -312,17 +312,17 @@
         cot_turned = buf[1, here, out_cols].T
 
         def tile(n, carry):
-            at = pl.ds(pl.multiple_of(n * 256, 256), 256)
+            at = pl.ds(pl.multiple_of(n * 512, 512), 512)
             d_hidden = jnp.dot(buf[1, here, :], wout[:, at], preferred_element_type=jnp.float32)
-            d_pre = (d_hidden * slope_g[:, :, at].reshape(chunk, 256)).astype(jnp.bfloat16)
+            d_pre = (d_hidden * slope_g[:, :, at].reshape(chunk, 512)).astype(jnp.bfloat16)
             acc_in[:, at] += jnp.dot(turned, d_pre, preferred_element_type=jnp.float32)
             acc_out[:, at] += jnp.dot(
-                cot_turned, hidden_g[:, :, at].reshape(chunk, 256),
+                cot_turned, hidden_g[:, :, at].reshape(chunk, 512),
                 preferred_element_type=jnp.float32,
             )
             return carry
 
-        lax.fori_loop(0, width // 256, tile, 0)
+        lax.fori_loop(0, width // 512, tile, 0)
         return carry
 
     lax.fori_loop(half, events, backward, 0)

time: 117 us -> 112 us (0.957)
  Pallas kernels: 110 us -> 105 us
    pallas_call x1, Pallas kernels: 110 us -> 105 us  [gathered_body(): pl.pallas_call(functools.partial(gather_kernel, chunk, seg_len), out_shap...]
where the time goes in v1:
time: 112 us; the launch traced here: 111 us
  Pallas kernels  105 us (94%)
  local copies, waits for them, and re-layouts  5.12 us (5%)
    pallas_call x1, Pallas kernels, gathered_body(): pl.pallas_call(functools.partial(gather_kernel, chunk, seg_len), out_shap...  105 us
    unnamed x2, local copies, waits for them, and re-layouts  4.52 us

profile of v1, /device:TPU:1, one launch (start us, length us, event | category | flops | bytes accessed | tf_op | source)
XLA Modules:
  0.0 111.3 jit_solution(1049877178939374188)
XLA Ops:
  0.6 0.8 pad_add_fusion
  1.4 0.6 broadcast_in_dim.13.meta_ref
  2.0 104.7 %gathered_step.1 = (bf16[512,1024]{1,0:T(8,128)(2,1)}, bf16[512,1024]{1,0:T(8,128)(2,1)}) custom-call(s32[8,128]{1,0:T(8,128)} %broadcast_in_dim.13.meta_ref, f32[1,2048]{1,0:T(1,128)} %bitcast.4, bf16[512,512]{1,0:T(8,128)(2,1)} %bitcast.3, bf16[512,512]{1,0:T(8,128)(2,1)} %cot_ref.1, bf16[2048,1024]{1,0:T(8,128)(2,1)} %win_ref.1, bf16[2048,1024]{1,0:T(8,128)(2,1)} %wout_ref.1), custom_call_target="tpu_custom_call" | custom-call | tf_op jit(solution)/shard_map/gathered_step/pallas_call | solution.py:358
  106.7 2.3 %copy.12 = bf16[512,1024]{1,0:T(8,128)(2,1)} copy(bf16[512,1024]{1,0:T(8,128)(2,1)} %get-tuple-element.4) | data formatting | bytes 2097152
  109.0 2.3 %copy.13 = bf16[512,1024]{1,0:T(8,128)(2,1)} copy(bf16[512,1024]{1,0:T(8,128)(2,1)} %get-tuple-element.5) | data formatting | bytes 2097152
  (1 shorter events, 0.0 us)

commit v2 on v1

--- a/solution.py
+++ b/solution.py
@@ -261,7 +261,7 @@
         normed_r[pl.ds(seg0, chunk_segs)] = normed_t[:, out_cols].reshape(chunk_segs, seg_len, cols)
 
         def tile(n, carry):
-            at = pl.ds(pl.multiple_of(n * 512, 512), 512)
+            at = pl.ds(pl.multiple_of(n * 1024, 1024), 1024)
             u = jnp.dot(normed_t[...], win[:, at], preferred_element_type=jnp.float32)
             weight = wt[:, :1]
             square = u * u
@@ -271,11 +271,11 @@
                 1.0 + u * (1.0 - tangent) * (root_two_over_pi * (1.0 + 3.0 * 0.044715 * square))
             )
             hidden = (upper * u).astype(jnp.bfloat16)
-            hidden_r[pl.ds(seg0, chunk_segs), :, at] = hidden.reshape(chunk_segs, seg_len, 512)
-            slope_r[pl.ds(seg0, chunk_segs), :, at] = slope.reshape(chunk_segs, seg_len, 512)
+            hidden_r[pl.ds(seg0, chunk_segs), :, at] = hidden.reshape(chunk_segs, seg_len, 1024)
+            slope_r[pl.ds(seg0, chunk_segs), :, at] = slope.reshape(chunk_segs, seg_len, 1024)
             return carry
 
-        lax.fori_loop(0, width // 512, tile, 0)
+        lax.fori_loop(0, width // 1024, tile, 0)
         return carry
 
     lax.fori_loop(0, half, forward, 0)
@@ -312,22 +312,23 @@
         cot_turned = buf[1, here, out_cols].T
 
         def tile(n, carry):
-            at = pl.ds(pl.multiple_of(n * 512, 512), 512)
+            at = pl.ds(pl.multiple_of(n * 1024, 1024), 1024)
             d_hidden = jnp.dot(buf[1, here, :], wout[:, at], preferred_element_type=jnp.float32)
-            d_pre = (d_hidden * slope_g[:, :, at].reshape(chunk, 512)).astype(jnp.bfloat16)
+            d_pre = (d_hidden * slope_g[:, :, at].reshape(chunk, 1024)).astype(jnp.bfloat16)
             acc_in[:, at] += jnp.dot(turned, d_pre, preferred_element_type=jnp.float32)
             acc_out[:, at] += jnp.dot(
-                cot_turned, hidden_g[:, :, at].reshape(chunk, 512),
+                cot_turned, hidden_g[:, :, at].reshape(chunk, 1024),
                 preferred_element_type=jnp.float32,
             )
             return carry
 
-        lax.fori_loop(0, width // 512, tile, 0)
+        lax.fori_loop(0, width // 1024, tile, 0)
         return carry
 
     lax.fori_loop(half, events, backward, 0)
-    gin_ref[...] = (acc_in[...] / largest).astype(jnp.bfloat16)
-    gout_ref[...] = (acc_out[...] / largest).astype(jnp.bfloat16)
+    inverse = 1.0 / jnp.full((1, 128), largest, jnp.float32)[:, :1]
+    gin_ref[...] = (acc_in[...] * inverse).astype(jnp.bfloat16)
+    gout_ref[...] = (acc_out[...] * inverse).astype(jnp.bfloat16)
 
     def settle(e, carry):
         finish(e)

time: 112 us -> 111 us (level)
  no operation moved by 1% of the time
where the time goes in v2:
time: 111 us
  Pallas kernels  104 us (94%)
  local copies, waits for them, and re-layouts  5.12 us (5%)
    pallas_call x1, Pallas kernels, gathered_body(): pl.pallas_call(functools.partial(gather_kernel, chunk, seg_len), out_shap...  104 us
    unnamed x2, local copies, waits for them, and re-layouts  4.52 us

profile of v2, /device:TPU:1, one launch (start us, length us, event | category | flops | bytes accessed | tf_op | source)
XLA Modules:
  0.0 110.6 jit_solution(10770922127770496191)
XLA Ops:
  0.6 0.8 pad_add_fusion
  1.4 0.6 broadcast_in_dim.13.meta_ref
  2.0 104.1 %gathered_step.1 = (bf16[512,1024]{1,0:T(8,128)(2,1)}, bf16[512,1024]{1,0:T(8,128)(2,1)}) custom-call(s32[8,128]{1,0:T(8,128)} %broadcast_in_dim.13.meta_ref, f32[1,2048]{1,0:T(1,128)} %bitcast.4, bf16[512,512]{1,0:T(8,128)(2,1)} %bitcast.3, bf16[512,512]{1,0:T(8,128)(2,1)} %cot_ref.1, bf16[2048,1024]{1,0:T(8,128)(2,1)} %win_ref.1, bf16[2048,1024]{1,0:T(8,128)(2,1)} %wout_ref.1), custom_call_target="tpu_custom_call" | custom-call | tf_op jit(solution)/shard_map/gathered_step/pallas_call | solution.py:359
  106.1 2.3 %copy.12 = bf16[512,1024]{1,0:T(8,128)(2,1)} copy(bf16[512,1024]{1,0:T(8,128)(2,1)} %get-tuple-element.4) | data formatting | bytes 2097152
  108.3 2.3 %copy.13 = bf16[512,1024]{1,0:T(8,128)(2,1)} copy(bf16[512,1024]{1,0:T(8,128)(2,1)} %get-tuple-element.5) | data formatting | bytes 2097152
  (1 shorter events, 0.0 us)
